TPU v7x, 128 devices: a whole 4x4x4 slice. The times are simulated.
128 devices in a mesh: wide: 16 (over x, y_hi, core), narrow: 8 (over y_lo, z).
Axes of the slice: x: 4, y: 4 (y_hi: 2, y_lo: 2; y = y_hi * 2 + y_lo), z: 4, core: 2. Of those that a mesh axis runs over, the one named last changes fastest.
Arguments:
- voltages: bfloat16 [2048, 262144], P('wide', 'narrow'), as said below
Outputs:
- visibility: float32 [128, 2048, 2048], P(('wide', 'narrow'))
Inputs may be any that keep to these rules, and one draw needn't show every extreme that they name: Real voltages; the power of an input may vary over the window.
All inputs are finite; a program needn't handle non-finite values.
Results may differ from a plain program's by a relative error of at most 0.0013.
Values may be sent and summed in bfloat16 or wider, within the bound.
A program may use at most 128 MiB of HBM per device.

v0:
```python
import math

import jax
import jax.numpy as jnp
from jax import lax
from jax.sharding import PartitionSpec as P

S = 2048
L = 512
TAPS = 4
CH_DEV = 1
FR_DEV = 64


def shifted(block, axis, distance):
    devices = range(lax.axis_size(axis))
    route = [(i - distance, i) for i in devices if i - distance in devices]
    return lax.ppermute(block, axis, route)


def channel_table(count):
    index = jnp.arange(L, dtype=jnp.int32)[:, None]
    channel = jnp.arange(count, dtype=jnp.int32)[None, :]
    angle = (index * channel % L).astype(jnp.float32) * (2.0 * math.pi / L)
    return jnp.concatenate([jnp.cos(angle), -jnp.sin(angle)], axis=1).astype(jnp.bfloat16)


def taper_table():
    place = jnp.arange(TAPS * L, dtype=jnp.float32)
    offset = (place - TAPS * L / 2.0 + 0.5) / L
    window = 0.5 - 0.5 * jnp.cos(2.0 * math.pi * (place + 0.5) / (TAPS * L))
    return (jnp.sinc(offset) * window).reshape(TAPS, L)


def filter_frames(frames, taper):
    count = frames.shape[1] - TAPS + 1
    total = jnp.zeros((frames.shape[0], count, L), jnp.float32)
    for step in range(TAPS):
        total = total + frames[:, step : step + count, :].astype(jnp.float32) * taper[step]
    return total.astype(jnp.bfloat16)


def pair_product(left, right):
    return lax.dot_general(
        left, right, (((1,), (1,)), ((), ())), preferred_element_type=jnp.float32
    )


def body(voltages):
    inputs = voltages.shape[0]
    width = lax.axis_size("wide")
    depth = lax.axis_size("narrow")
    chan = CH_DEV * width * depth
    frames_all = FR_DEV * depth
    history = shifted(voltages[:, voltages.shape[1] - (TAPS - 1) * L :], "narrow", 1)
    padded = jnp.concatenate([history, voltages], axis=1).reshape(inputs, FR_DEV + TAPS - 1, L)
    filtered = filter_frames(padded, taper_table())
    spectrum = jnp.dot(
        filtered.reshape(inputs * FR_DEV, L),
        channel_table(chan),
        preferred_element_type=jnp.float32,
    )
    spectrum = spectrum.reshape(inputs, FR_DEV, 2 * chan)
    total = lax.psum(jnp.sum(spectrum * spectrum, axis=1), "narrow")
    power = (total[:, :chan] + total[:, chan:]) / frames_all
    factor = 1.0 / jnp.sqrt(power + 1e-06)
    factor = jnp.concatenate([factor, factor], axis=1)
    requantized = (spectrum * factor[:, None, :]).astype(jnp.bfloat16)
    outgoing = requantized.reshape(1, inputs, FR_DEV, 2, chan)
    arrived = lax.all_to_all(outgoing, ("wide", "narrow"), split_axis=4, concat_axis=0, tiled=True)
    arrived = arrived.reshape(width, depth, inputs, FR_DEV, 2, CH_DEV)
    ordered = jnp.transpose(arrived, (5, 0, 2, 4, 1, 3))
    ordered = ordered.reshape(CH_DEV, S, 2 * frames_all)
    joined = ordered[0]
    turned = jnp.concatenate([joined[:, frames_all:], -joined[:, :frames_all]], axis=1)
    row = lax.broadcasted_iota(jnp.int32, (S, S), 0)
    col = lax.broadcasted_iota(jnp.int32, (S, S), 1)
    real_part = pair_product(joined, joined)
    imag_part = pair_product(turned, joined)
    results = [jnp.where(row >= col, real_part, imag_part) / frames_all]
    return jnp.stack(results, axis=0)


def solution(mesh):
    placed = (P("wide", "narrow"),)
    return jax.shard_map(
        body,
        mesh=mesh,
        in_specs=placed,
        out_specs=P(("wide", "narrow"), None, None),
        check_vma=False,
    )
```

profile of v0, /device:TPU:1, one launch (start us, length us, event | category | flops | bytes accessed | tf_op | source)
XLA Modules:
  0.0 266.9 jit_solution(6769377799326997830)
XLA Ops:
  6.5 0.0 all-reduce.2.cloned.1.call-start
  6.5 11.9 %copy.11 = bf16[128,32768]{0,1:T(8,128)(2,1)} copy(bf16[128,32768]{1,0:T(8,128)(2,1)} %param.1) | data formatting | bytes 16777216 | tf_op args[0]
  18.5 1.0 slice.56
  19.5 4.4 %collective-permute-start = (bf16[128,1536]{0,1:T(8,128)(2,1)S(1)}, bf16[128,1536]{0,1:T(8,128)(2,1)S(1)}, u32[]{:S(2)}, u32[]{:S(2)}) collective-permute-start(bf16[128,1536]{0,1:T(8,128)(2,1)S(1)} %slice.56), channel_id=1, source_target_pairs={{0,1},{1,2},{2,3},{3,4},{4,5},{5,6},{6,7},{8,9},{9,10},{10,11},{11... | collective-permute-start | bytes 1179656 | tf_op jit(solution)/shard_map/ppermute | solution.py:18
  23.9 0.1 fusion.19
  24.0 1.1 negate_convert_fusion
  25.1 6.6 %collective-permute-done = bf16[128,1536]{0,1:T(8,128)(2,1)S(1)} collective-permute-done((bf16[128,1536]{0,1:T(8,128)(2,1)S(1)}, bf16[128,1536]{0,1:T(8,128)(2,1)S(1)}, u32[]{:S(2)}, u32[]{:S(2)}) %collective-permute-start) | collective-permute-done | bytes 393248 | tf_op jit(solution)/shard_map/ppermute | solution.py:18
  31.6 10.7 %pad_maximum_fusion = bf16[128,34304]{0,1:T(8,128)(2,1)} fusion(bf16[128,32768]{0,1:T(8,128)(2,1)} %copy.11, bf16[128,1536]{0,1:T(8,128)(2,1)S(1)} %collective-permute-done), kind=kLoop, calls=%fused_computation.3 | loop fusion | flops 17563648 | bytes 17563648 | tf_op jit(solution)/shard_map/concatenate | solution.py:56
  42.3 17.1 %multiply_reduce_fusion = (f32[128,256]{1,0:T(8,128)}, f32[128,64,256]{2,0,1:T(8,128)}) fusion(bf16[512,128]{1,0:T(8,128)(2,1)S(1)} %get-tuple-element.13, bf16[512,128]{1,0:T(8,128)(2,1)S(1)} %get-tuple-element.14, bf16[128,67,512]{0,2,1:T(8,128)(2,1)} %bitcast.31, f32[512]{0:T(512)S(1)} %get-tuple-element.8, f32[512]{0:T(512)S(1)} %get-tuple-element.9, ...), kind=kOutput, calls=%fused_computation.5 | convolution fusion | flops 2202501120 | bytes 42344448 | tf_op jit(solution)/shard_map/dot_general | solution.py:58
  59.4 0.0 all-reduce.2.cloned.1.call-update
  59.5 72.6 %all-reduce.2.cloned.1.call-done = f32[128,256]{1,0:T(8,128)} async-done(((f32[128,256]{1,0:T(8,128)}), f32[128,256]{1,0:T(8,128)}) %all-reduce.2.cloned.1.call-update) | async-done | bytes 131088 | tf_op jit(solution)/shard_map/psum | solution.py:64
  132.1 0.9 fusion.14
  133.0 6.5 %multiply_convert_fusion = bf16[128,64,256]{2,0,1:T(8,128)(2,1)} fusion(f32[128,64,256]{2,0,1:T(8,128)} %get-tuple-element.12, f32[128,256]{1,0:T(8,128)S(1)} %pad_maximum_fusion.1), kind=kLoop, calls=%fused_computation.4 | loop fusion | flops 4194304 | bytes 12713984 | tf_op jit(solution)/shard_map/convert_element_type | solution.py:68
  139.5 6.9 %reshape.29 = bf16[1,128,64,2,128]{4,3,1,2,0:T(2,128)(2,1)} reshape(bf16[128,64,256]{2,0,1:T(8,128)(2,1)} %multiply_convert_fusion) | data formatting | bytes 8388608 | tf_op jit(solution)/shard_map/reshape | solution.py:69
  146.4 8.2 %copy.14 = bf16[1,128,64,2,128]{1,2,3,0,4:T(8,128)(2,1)} copy(bf16[1,128,64,2,128]{4,3,1,2,0:T(2,128)(2,1)} %reshape.29) | data formatting | bytes 8388608 | tf_op jit(solution)/shard_map/reshape | solution.py:69
  154.6 65.3 %all_to_all.15 = bf16[1,128,64,2,128]{1,2,3,0,4:T(8,128)(2,1)S(1)} all-to-all(bf16[1,128,64,2,128]{1,2,3,0,4:T(8,128)(2,1)} %copy.14), channel_id=1, replica_groups=mesh['wide'=16,'narrow'=8] {'wide','narrow'}, dimensions={4} | all-to-all | bytes 8388608 | tf_op jit(solution)/shard_map/all_to_all | solution.py:70
  219.9 3.5 %copy.15 = bf16[1,16,128,2,8,64]{2,1,5,4,3,0:T(8,128)(2,1)S(1)} copy(bf16[1,16,128,2,8,64]{2,5,0,3,4,1:T(8,128)(2,1)S(1)} %bitcast.30) | data formatting | bytes 8388608 | tf_op jit(solution)/shard_map/transpose | solution.py:72
  223.4 2.1 copy.21
  225.5 14.9 %fusion.46 = f32[2048,2048]{1,0:T(8,128)} fusion(bf16[128,8,16,128]{3,2,1,0:T(8,128)(2,1)S(1)} %bitcast.27), kind=kOutput, calls=%fused_computation.70 | convolution fusion | flops 8589934592 | bytes 20971520 | tf_op jit(solution)/shard_map/dot_general | solution.py:44
  240.4 1.6 fusion.47
  242.0 18.0 %multiply_bitcast_fusion = f32[1,2048,2048]{2,1,0:T(8,128)} fusion(f32[2048,2048]{1,0:T(8,128)} %fusion.46, bf16[2048,512]{0,1:T(8,128)(2,1)} %get-tuple-element.6, bf16[2048,512]{0,1:T(8,128)(2,1)S(1)} %get-tuple-element.5, bf16[128,8,16,128]{3,2,1,0:T(8,128)(2,1)S(1)} %bitcast.28), kind=kOutput, calls=%fused_computation | convolution fusion | flops 8610906112 | bytes 41943040 | tf_op jit(solution)/shard_map/dot_general | solution.py:44
  (2 shorter events, 0.0 us)
Async XLA Ops:
  6.5 125.5 %all-reduce.2.cloned.1.call-start = ((), (), s32[]{:S(2)}) async-start(), calls=%async_computation.1 | async-start | bytes 262144 | tf_op jit(solution)/shard_map/psum | solution.py:64
  19.5 12.1 %collective-permute-start = (bf16[128,1536]{0,1:T(8,128)(2,1)S(1)}, bf16[128,1536]{0,1:T(8,128)(2,1)S(1)}, u32[]{:S(2)}, u32[]{:S(2)}) collective-permute-start(bf16[128,1536]{0,1:T(8,128)(2,1)S(1)} %slice.56), channel_id=1, source_target_pairs={{0,1},{1,2},{2,3},{3,4},{4,5},{5,6},{6,7},{8,9},{9,10},{10,11},{11... | collective-permute-start | bytes 1179656 | tf_op jit(solution)/shard_map/ppermute | solution.py:18
Sparse Core Ops, SparseCore 0:
  59.6 72.4 all-reduce.1
where the time goes:
time: 268 us; the launch traced here: 267 us
  waiting for transfers between devices  79.2 us (30%)
  blocking collectives  65.3 us (24%)
  matrix products  50 us (19%)
  local copies, waits for them, and re-layouts  33.7 us (13%)
  other arithmetic  20.8 us (8%)
  between operations  13.4 us (5%)
  starting transfers between devices  4.4 us (2%)
    psum x1, waiting for transfers between devices, body(): total = lax.psum(jnp.sum(spectrum * spectrum, axis=1), 'narrow')  72.6 us
    all_to_all x1, blocking collectives, body(): lax.all_to_all(outgoing, ('wide', 'narrow'), split_axis=4, concat_axis=0,...  65.3 us
    dot_general x2, matrix products, pair_product(): lax.dot_general(left, right, (((1,), (1,)), ((), ())), preferred_element_...  32.9 us
    dot_general x1, matrix products, body(): jnp.dot(filtered.reshape(inputs * FR_DEV, L), channel_table(chan), prefer...  17.1 us
    reshape x2, local copies, waits for them, and re-layouts, body(): outgoing = requantized.reshape(1, inputs, FR_DEV, 2, chan)  15.1 us
    unnamed x2, local copies, waits for them, and re-layouts  14.1 us
    concatenate x1, other arithmetic, body(): jnp.concatenate([history, voltages], axis=1)  10.7 us
    ppermute x1, waiting for transfers between devices, shifted(): return lax.ppermute(block, axis, route)  6.55 us
  transfers between devices with their start and end apart: 2, of which 2 were waited for; matrix products, arithmetic and copies ran while one was open for 0% of the time, Pallas kernels for 0%

commit v1 on v0

v1 whole, which is shorter than its diff:
```python
import functools
import math

import jax
import jax.numpy as jnp
from jax import lax
from jax.experimental import pallas as pl
from jax.experimental.pallas import tpu as pltpu
from jax.sharding import PartitionSpec as P

S = 2048
L = 512
TAPS = 4
CHAN = 128
FRAMES = 512
WIDE = 16
NARROW = 8
ROWS = S // WIDE
FR_DEV = FRAMES // NARROW
HIST = (TAPS - 1) * L
STEP = 16
CHUNKS = FR_DEV // STEP
ORDER = (1, 2, 3, 0)
KB = 2 * STEP * NARROW
TILE = 256
MESH = pl.DeviceIdType.MESH


def channel_table(count):
    index = jnp.arange(L, dtype=jnp.int32)[:, None]
    channel = jnp.arange(count, dtype=jnp.int32)[None, :]
    angle = (index * channel % L).astype(jnp.float32) * (2.0 * math.pi / L)
    return jnp.concatenate([jnp.cos(angle), -jnp.sin(angle)], axis=1).astype(jnp.bfloat16)


def taper_table():
    place = jnp.arange(TAPS * L, dtype=jnp.float32)
    offset = (place - TAPS * L / 2.0 + 0.5) / L
    window = 0.5 - 0.5 * jnp.cos(2.0 * math.pi * (place + 0.5) / (TAPS * L))
    return (jnp.sinc(offset) * window).reshape(TAPS, L)


def exchange(
    x_hbm, taper, table, k_out, turned, j_out, power, factor_col,
    xv, filt, spec, w, load_sem, hist_send, hist_recv, send_sem, recv_sem,
):
    wide = lax.axis_index("wide")
    narrow = lax.axis_index("narrow")
    x, y, z, core = wide // 4, (wide // 2) % 2 * 2 + narrow // 4, narrow % 4, wide % 2
    mine = wide * NARROW + narrow

    def partner(step):
        offset = (37 * step) % 128
        px = (x + (offset // 2) % 4) % 4
        py = (y + (offset // 8) % 4) % 4
        pz = (z + offset // 32) % 4
        pc = (core + offset % 2) % 2
        return px * 4 + py // 2 * 2 + pc, py % 2 * 4 + pz

    barrier = pltpu.get_barrier_semaphore()

    def greet(step, carry):
        pl.semaphore_signal(barrier, inc=1, device_id=partner(step), device_id_type=MESH)
        return carry

    lax.fori_loop(1, 128, greet, 0)

    loads = []
    ready = 0
    pieces = [(STEP - 3, 2 * STEP), (2 * STEP, 3 * STEP), (3 * STEP, 4 * STEP), (0, STEP - 3)]
    for index, (first, last) in enumerate(pieces):
        copy = pltpu.make_async_copy(
            x_hbm.at[:, first * L : last * L],
            xv.at[:, (first + 3) * L : (last + 3) * L],
            load_sem.at[index],
        )
        copy.start()
        loads.append(copy)

    history = pltpu.make_async_remote_copy(
        x_hbm.at[:, FR_DEV * L - HIST :],
        xv.at[:, :HIST],
        hist_send,
        hist_recv,
        device_id=(wide, (narrow + 1) % NARROW),
        device_id_type=MESH,
    )

    def compute(g):
        def pair(p, carry):
            for half in range(2):
                base = (g * STEP + 2 * p + half) * L
                for r in range(0, ROWS, 16):
                    total = None
                    for tap in range(TAPS):
                        part = xv[r : r + 16, pl.ds(pl.multiple_of(base + tap * L, L), L)]
                        term = part.astype(jnp.float32) * taper[tap : tap + 1, :]
                        total = term if total is None else total + term
                    filt[half * ROWS + r : half * ROWS + r + 16, :] = total.astype(jnp.bfloat16)
            out = lax.dot_general(
                table[...], filt[...], (((1,), (1,)), ((), ())), preferred_element_type=jnp.float32
            )
            row = pl.multiple_of(p * (2 * 2 * CHAN), 2 * 2 * CHAN)
            spec[pl.ds(row, 2 * CHAN), :] = out[:, :ROWS]
            spec[pl.ds(row + 2 * CHAN, 2 * CHAN), :] = out[:, ROWS:]
            return carry

        lax.fori_loop(0, STEP // 2, pair, 0)

        def turn(c, carry):
            re = spec[pl.ds(c, STEP, stride=2 * CHAN), :]
            im = spec[pl.ds(c + CHAN, STEP, stride=2 * CHAN), :]
            w[g, c] = jnp.concatenate([re, im], axis=0).astype(jnp.bfloat16)
            return carry

        lax.fori_loop(0, CHAN, turn, 0)

    def send(g):
        row = pl.multiple_of(narrow * (2 * STEP), 2 * STEP)
        col = pl.multiple_of(wide * ROWS, ROWS)
        dst = k_out.at[g, pl.ds(row, 2 * STEP), pl.ds(col, ROWS)]

        def one(step, carry):
            pw, pn = partner(step)
            pltpu.make_async_remote_copy(
                w.at[g, pw * NARROW + pn],
                dst,
                send_sem,
                recv_sem.at[g],
                device_id=(pw, pn),
                device_id_type=MESH,
            ).start()
            return carry

        lax.fori_loop(1, 128, one, 0)
        pltpu.make_async_copy(w.at[g, mine], dst, recv_sem.at[g]).start()

    for index, g in enumerate(ORDER):
        loads[index].wait()
        if g == 0:
            @pl.when(narrow > 0)
            def _():
                history.wait_recv()

        compute(g)
        if index == 0:
            pl.semaphore_wait(barrier, 127)

            @pl.when(narrow == 0)
            def _():
                xv[:, :HIST] = jnp.zeros((ROWS, HIST), jnp.bfloat16)

            @pl.when(narrow < NARROW - 1)
            def _():
                history.start()

        send(g)

    for index, g in enumerate(ORDER):
        pltpu.make_async_copy(k_out.at[g], k_out.at[g], recv_sem.at[g]).wait()

        def block(b, carry):
            cols = pl.ds(pl.multiple_of(b * TILE, TILE), TILE)
            value = k_out[g, :, cols]
            j_out[g, cols, :] = value.T
            sums = jnp.zeros((1, TILE), jnp.float32)
            for r in range(0, KB, 2 * STEP):
                re = value[r : r + STEP, :]
                im = value[r + STEP : r + 2 * STEP, :]
                turned[g, r : r + 2 * STEP, cols] = jnp.concatenate([-im, re], axis=0)
                both = value[r : r + 2 * STEP, :].astype(jnp.float32)
                sums = sums + jnp.sum(both * both, axis=0, keepdims=True)
            if index == 0:
                power[:, cols] = sums
            else:
                power[:, cols] = power[:, cols] + sums
            return carry

        lax.fori_loop(0, S // TILE, block, 0)

    factor = 1.0 / jnp.sqrt(power[...] / FRAMES + 1e-06)
    power[...] = factor
    for b in range(0, S, 128):
        factor_col[b : b + 128, :] = jnp.broadcast_to(factor[:, b : b + 128], (128, 128)).T

    @pl.when(narrow < NARROW - 1)
    def _():
        history.wait_send()

    for g in range(CHUNKS):
        part = w.at[g, pl.ds(0, 127)]
        pltpu.make_async_copy(part, part, send_sem).wait()


def correlate(k, turned, j, factor_row, factor_col, out, stage, sem):
    def rows(i, slot, wait):
        @pl.when(wait)
        def _():
            pltpu.make_async_copy(stage.at[slot], out.at[0, pl.ds(0, TILE), :], sem.at[slot]).wait()

        r = pl.ds(pl.multiple_of(i * TILE, TILE), TILE)
        left = [j[g, r, :] for g in range(CHUNKS)]
        scale = jnp.tile(factor_col[r, :], (1, TILE // 128)) * (1.0 / FRAMES)

        def product(right, cols):
            total = None
            for g in range(CHUNKS):
                term = jnp.dot(left[g], right[g, :, cols], preferred_element_type=jnp.float32)
                total = term if total is None else total + term
            return total * scale * factor_row[:, cols]

        def column(c, carry):
            cols = pl.ds(pl.multiple_of(c * TILE, TILE), TILE)

            @pl.when(c < i)
            def _():
                stage[slot, :, cols] = product(k, cols)

            @pl.when(c > i)
            def _():
                stage[slot, :, cols] = product(turned, cols)

            @pl.when(c == i)
            def _():
                row = lax.broadcasted_iota(jnp.int32, (TILE, TILE), 0)
                col = lax.broadcasted_iota(jnp.int32, (TILE, TILE), 1)
                stage[slot, :, cols] = jnp.where(row >= col, product(k, cols), product(turned, cols))

            return carry

        lax.fori_loop(0, S // TILE, column, 0)
        pltpu.make_async_copy(stage.at[slot], out.at[0, r, :], sem.at[slot]).start()

    def both(p, carry):
        rows(2 * p, 0, p > 0)
        rows(2 * p + 1, 1, p > 0)
        return carry

    lax.fori_loop(0, S // TILE // 2, both, 0)
    for slot in range(2):
        pltpu.make_async_copy(stage.at[slot], out.at[0, pl.ds(0, TILE), :], sem.at[slot]).wait()


def body(voltages):
    vmem = pl.BlockSpec(memory_space=pltpu.VMEM)
    hbm = pl.BlockSpec(memory_space=pl.ANY)
    dma = pltpu.SemaphoreType.DMA
    k, turned, j, power, factor_col = pl.pallas_call(
        exchange,
        out_shape=[
            pltpu.VMEM((CHUNKS, KB, S), jnp.bfloat16),
            pltpu.VMEM((CHUNKS, KB, S), jnp.bfloat16),
            pltpu.VMEM((CHUNKS, S, KB), jnp.bfloat16),
            pltpu.VMEM((1, S), jnp.float32),
            pltpu.VMEM((S, 128), jnp.float32),
        ],
        in_specs=[hbm, vmem, vmem],
        out_specs=[vmem] * 5,
        scratch_shapes=[
            pltpu.VMEM((ROWS, (FR_DEV + TAPS - 1) * L), jnp.bfloat16),
            pltpu.VMEM((2 * ROWS, L), jnp.bfloat16),
            pltpu.VMEM((STEP * 2 * CHAN, ROWS), jnp.float32),
            pltpu.VMEM((CHUNKS, CHAN, 2 * STEP, ROWS), jnp.bfloat16),
            dma((CHUNKS,)),
            dma,
            dma,
            dma,
            dma((CHUNKS,)),
        ],
        compiler_params=pltpu.CompilerParams(
            collective_id=0, has_side_effects=True, vmem_limit_bytes=34 << 20
        ),
        name="exchange",
    )(voltages, taper_table(), channel_table(CHAN).T)
    return pl.pallas_call(
        correlate,
        out_shape=jax.ShapeDtypeStruct((1, S, S), jnp.float32),
        in_specs=[vmem] * 5,
        out_specs=hbm,
        scratch_shapes=[pltpu.VMEM((2, TILE, S), jnp.float32), dma((2,))],
        compiler_params=pltpu.CompilerParams(vmem_limit_bytes=34 << 20),
        name="correlate",
    )(k, turned, j, power, factor_col)


def solution(mesh):
    return jax.shard_map(
        body,
        mesh=mesh,
        in_specs=(P("wide", "narrow"),),
        out_specs=P(("wide", "narrow"), None, None),
        check_vma=False,
    )
```

time: 268 us -> 112 us (0.42)
  Pallas kernels: 0 us -> 108 us
  waiting for transfers between devices: 79.2 us -> 0 us
  blocking collectives: 65.3 us -> 0 us
  matrix products: 50 us -> 0 us
  local copies, waits for them, and re-layouts: 33.7 us -> 0 us
  other arithmetic: 20.8 us -> 1.21 us
  between operations: 13.4 us -> 0.03 us
  starting transfers between devices: 4.4 us -> 0 us
    pallas_call x0 -> x2, Pallas kernels: none -> 108 us  [the longest x1 84.6 us: body(): pl.pallas_call(exchange, out_shape=[pltpu.VMEM((CHUNKS, KB, S), jnp.bfloa...]
    psum x1 -> x0, waiting for transfers between devices: 72.6 us -> none  [body(): total = lax.psum(jnp.sum(spectrum * spectrum, axis=1), 'narrow')]
    all_to_all x1 -> x0, blocking collectives: 65.3 us -> none  [body(): lax.all_to_all(outgoing, ('wide', 'narrow'), split_axis=4, concat_axis=0,...]
    dot_general x3 -> x0, matrix products: 50 us -> none  [the longest x2 32.9 us: pair_product(): lax.dot_general(left, right, (((1,), (1,)), ((), ())), preferred_element_...]
    reshape x2 -> x0, local copies, waits for them, and re-layouts: 15.1 us -> none  [body(): outgoing = requantized.reshape(1, inputs, FR_DEV, 2, chan)]
    unnamed x2 -> x0, local copies, waits for them, and re-layouts: 14.1 us -> none
    concatenate x2 -> x0, other arithmetic: 10.7 us -> none  [the longest x1 10.7 us: body(): jnp.concatenate([history, voltages], axis=1)]
    ppermute x1 -> x0, waiting for transfers between devices: 6.55 us -> none  [shifted(): return lax.ppermute(block, axis, route)]
  transfers between devices with their start and end apart: 2 -> 0, of which waited for: 2 -> 0; matrix products, arithmetic and copies ran while one was open for 0% -> 0% of each run, Pallas kernels for 0% -> 0%
where the time goes in v1:
time: 112 us; the launch traced here: 110 us
  Pallas kernels  108 us (96%)
  other arithmetic  1.21 us (1%)
    pallas_call x1, Pallas kernels, body(): pl.pallas_call(exchange, out_shape=[pltpu.VMEM((CHUNKS, KB, S), jnp.bfloa...  84.6 us
    pallas_call x1, Pallas kernels, body(): pl.pallas_call(correlate, out_shape=jax.ShapeDtypeStruct((1, S, S), jnp.f...  23.7 us

profile of v1, /device:TPU:1, one launch (start us, length us, event | category | flops | bytes accessed | tf_op | source)
XLA Modules:
  0.0 109.5 jit_solution(12203106611870060365)
XLA Ops:
  0.0 0.1 fusion.11.taper
  0.1 1.1 %negate_convert_fusion = (bf16[512,128]{0,1:T(8,128)(2,1)S(1)}, bf16[512,128]{0,1:T(8,128)(2,1)S(1)}) fusion(), kind=kLoop, calls=%fused_computation.7 | loop fusion | flops 1114112 | bytes 262144 | tf_op jit(solution)/shard_map/convert.1
  1.2 84.6 %exchange.1 = (bf16[4,256,2048]{2,1,0:T(8,128)(2,1)S(1)}, bf16[4,256,2048]{2,1,0:T(8,128)(2,1)S(1)}, bf16[4,2048,256]{2,1,0:T(8,128)(2,1)S(1)}, f32[1,2048]{1,0:T(1,128)S(1)}, f32[2048,128]{1,0:T(8,128)S(1)}) custom-call(bf16[128,32768]{1,0:T(8,128)(2,1)} %x_hbm.1, f32[4,512]{1,0:T(4,128)S(1)} %fusion.11.taper, bf16[256,512]{1,0:T(8,128)(2,1)S(1)} %maximum_bitcast_fusion.table), custom_call_target="tpu_custom_call" | custom-call | tf_op jit(solution)/shard_map/exchange/pallas_call | solution.py:248
  85.8 23.7 %correlate.1 = f32[1,2048,2048]{2,1,0:T(8,128)} custom-call(bf16[4,256,2048]{2,1,0:T(8,128)(2,1)S(1)} %get-tuple-element.10.k, bf16[4,256,2048]{2,1,0:T(8,128)(2,1)S(1)} %get-tuple-element.11.turned, bf16[4,2048,256]{2,1,0:T(8,128)(2,1)S(1)} %get-tuple-element.12.j, f32[1,2048]{1,0:T(1,128)S(1)} %get-tuple-element.13.factor_row, ...), custom_call_target="tpu_custom_call" | custom-call | tf_op jit(solution)/shard_map/correlate/pallas_call | solution.py:275
  (1 shorter events, 0.0 us)

commit v2 on v1

v2 whole, which is shorter than its diff:
```python
import functools
import math

import jax
import jax.numpy as jnp
from jax import lax
from jax.experimental import pallas as pl
from jax.experimental.pallas import tpu as pltpu
from jax.sharding import PartitionSpec as P

S = 2048
L = 512
TAPS = 4
CHAN = 128
FRAMES = 512
WIDE = 16
NARROW = 8
ROWS = S // WIDE
FR_DEV = FRAMES // NARROW
STEP = 16
CHUNKS = FR_DEV // STEP
ORDER = (1, 2, 3, 0)
KB = 2 * STEP * NARROW
TILE = 256
MESH = pl.DeviceIdType.MESH


def channel_table(count):
    index = jnp.arange(L, dtype=jnp.int32)[:, None]
    channel = jnp.arange(count, dtype=jnp.int32)[None, :]
    angle = (index * channel % L).astype(jnp.float32) * (2.0 * math.pi / L)
    return jnp.concatenate([jnp.cos(angle), -jnp.sin(angle)], axis=1).astype(jnp.bfloat16)


def taper_table():
    place = jnp.arange(TAPS * L, dtype=jnp.float32)
    offset = (place - TAPS * L / 2.0 + 0.5) / L
    window = 0.5 - 0.5 * jnp.cos(2.0 * math.pi * (place + 0.5) / (TAPS * L))
    return (jnp.sinc(offset) * window).reshape(TAPS, L)


def products(i, left, right, emit):
    def dot(kind, cols):
        return jnp.dot(left, right[kind, :, cols], preferred_element_type=jnp.float32)

    def columns(c):
        return pl.ds(pl.multiple_of(c * TILE, TILE), TILE)

    for t in range(1, S // TILE):
        c = (i + t) % (S // TILE)
        emit(columns(c), dot(jnp.where(c > i, 1, 0), columns(c)))
    row = lax.broadcasted_iota(jnp.int32, (TILE, TILE), 0)
    col = lax.broadcasted_iota(jnp.int32, (TILE, TILE), 1)
    emit(columns(i), jnp.where(row >= col, dot(0, columns(i)), dot(1, columns(i))))


def exchange(
    x_hbm, taper, table, acc, last, last_j, power, factor_col,
    xv, filt, spec, w, kt, j, taper_edge, load_sem, hist_send, hist_recv, send_sem, recv_sem,
):
    wide = lax.axis_index("wide")
    narrow = lax.axis_index("narrow")
    x, y, z, core = wide // 4, (wide // 2) % 2 * 2 + narrow // 4, narrow % 4, wide % 2
    mine = wide * NARROW + narrow

    def partners(q):
        for step in range(4):
            dy = (q % 4 + step) % 4
            px = (x + step) % 4
            py = (y + dy) % 4
            pz = (z + q // 4 + dy + step) % 4
            for flip in range(2):
                pc = (core + flip) % 2
                yield step == 0 and flip == 0, (px * 4 + py // 2 * 2 + pc, py % 2 * 4 + pz)

    def everyone(q, visit):
        for own, device in partners(q):
            if own:
                pl.when(q > 0)(functools.partial(visit, device))
            else:
                visit(device)

    barrier = pltpu.get_barrier_semaphore()

    def greet(q, carry):
        def signal(device):
            pl.semaphore_signal(barrier, inc=1, device_id=device, device_id_type=MESH)

        everyone(q, signal)
        return carry

    lax.fori_loop(0, 16, greet, 0)

    loads = []
    pieces = [(STEP - 3, 2 * STEP), (2 * STEP, 3 * STEP), (3 * STEP, 4 * STEP), (0, STEP - 3)]
    for index, (first, end) in enumerate(pieces):
        copy = pltpu.make_async_copy(
            x_hbm.at[:, first * L : end * L],
            xv.at[:, (first + 2) * L : (end + 2) * L],
            load_sem.at[index],
        )
        copy.start()
        loads.append(copy)

    taper_edge[...] = taper[...] * jnp.where(
        (narrow == NARROW - 1) & (lax.broadcasted_iota(jnp.int32, (TAPS, L), 0) < TAPS - 1), 0.0, 1.0
    )

    def ahead(r):
        return pltpu.make_async_remote_copy(
            x_hbm.at[pl.ds(r, 16), (FR_DEV - 2) * L :],
            xv.at[pl.ds(r, 16), : 2 * L],
            hist_send.at[0],
            hist_recv.at[0],
            device_id=(wide, (narrow + 1) % NARROW),
            device_id_type=MESH,
        )

    def back(r):
        return pltpu.make_async_remote_copy(
            x_hbm.at[pl.ds(r, 16), :L],
            xv.at[pl.ds(r, 16), (FR_DEV + 2) * L :],
            hist_send.at[1],
            hist_recv.at[1],
            device_id=(wide, (narrow + NARROW - 1) % NARROW),
            device_id_type=MESH,
        )

    def compute(g):
        def filtered(slot, half, base, weights):
            for r in range(0, ROWS, 16):
                total = None
                for tap in range(TAPS):
                    part = xv[r : r + 16, pl.ds(pl.multiple_of(base + tap * L, L), L)]
                    term = part.astype(jnp.float32) * weights[tap : tap + 1, :]
                    total = term if total is None else total + term
                filt[slot, half * ROWS + r : half * ROWS + r + 16, :] = total.astype(jnp.bfloat16)

        def group(p, carry):
            for slot in range(2):
                for half in range(2):
                    f = g * STEP + 4 * p + 2 * slot + half
                    filtered(slot, half, jnp.maximum(f - 1, 0) * L, taper)
                if g == 0 and slot == 0:

                    @pl.when(p == 0)
                    def _():
                        filtered(0, 0, (FR_DEV - 1) * L, taper_edge)

                out = lax.dot_general(
                    table[...], filt[slot], (((1,), (1,)), ((), ())), preferred_element_type=jnp.float32
                )
                row = pl.multiple_of((4 * p + 2 * slot) * (2 * CHAN), 2 * 2 * CHAN)
                spec[pl.ds(row, 2 * CHAN), :] = out[:, :ROWS]
                spec[pl.ds(row + 2 * CHAN, 2 * CHAN), :] = out[:, ROWS:]
            return carry

        lax.fori_loop(0, STEP // 4, group, 0)

        def turn(b, carry):
            for c in range(8):
                re = spec[pl.ds(8 * b + c, STEP, stride=2 * CHAN), :]
                im = spec[pl.ds(8 * b + c + CHAN, STEP, stride=2 * CHAN), :]
                w[g, 8 * b + c] = jnp.concatenate([re, im], axis=0).astype(jnp.bfloat16)
            return carry

        lax.fori_loop(0, CHAN // 8, turn, 0)

    def landing(g):
        return kt.at[g - 1, 0] if g > 0 else last.at[0]

    def send(g, history):
        row = pl.multiple_of(narrow * (2 * STEP), 2 * STEP)
        col = pl.multiple_of(wide * ROWS, ROWS)
        dst = landing(g).at[pl.ds(row, 2 * STEP), pl.ds(col, ROWS)]

        def one(q, carry):
            if history:
                r = pl.multiple_of(q % 8 * 16, 16)

                @pl.when((narrow < NARROW - 1) & (q < 8))
                def _():
                    ahead(r).start()

                @pl.when(q >= 8)
                def _():
                    back(r).start()

            def start(device):
                pltpu.make_async_remote_copy(
                    w.at[g, device[0] * NARROW + device[1]],
                    dst,
                    send_sem,
                    recv_sem.at[g],
                    device_id=device,
                    device_id_type=MESH,
                ).start()

            everyone(q, start)
            return carry

        lax.fori_loop(0, 16, one, 0)
        pltpu.make_async_copy(w.at[g, mine], dst, recv_sem.at[g]).start()

    for index, g in enumerate(ORDER):
        loads[index].wait()
        if g == 0:
            before = xv.at[:, : 2 * L]
            after = xv.at[:, (FR_DEV + 2) * L :]

            @pl.when(narrow > 0)
            def _():
                pltpu.make_async_copy(before, before, hist_recv.at[0]).wait()

            pltpu.make_async_copy(after, after, hist_recv.at[1]).wait()

        compute(g)
        if index == 0:
            pl.semaphore_wait(barrier, 127)

            @pl.when(narrow == 0)
            def _():
                xv[:, : 2 * L] = jnp.zeros((ROWS, 2 * L), jnp.bfloat16)

        send(g, index == 0)

    for index, g in enumerate(ORDER):
        right = last if g == 0 else kt.at[g - 1]
        left = last_j if g == 0 else j
        pltpu.make_async_copy(right.at[0], right.at[0], recv_sem.at[g]).wait()

        def block(b, carry):
            cols = pl.ds(pl.multiple_of(b * TILE, TILE), TILE)
            value = right[0, :, cols]
            left[cols, :] = value.T
            sums = jnp.zeros((1, TILE), jnp.float32)
            for r in range(0, KB, 2 * STEP):
                re = value[r : r + STEP, :]
                im = value[r + STEP : r + 2 * STEP, :]
                right[1, r : r + 2 * STEP, cols] = jnp.concatenate([-im, re], axis=0)
                both = value[r : r + 2 * STEP, :].astype(jnp.float32)
                sums = sums + jnp.sum(both * both, axis=0, keepdims=True)
            if index == 0:
                power[:, cols] = sums
            else:
                power[:, cols] = power[:, cols] + sums
            return carry

        lax.fori_loop(0, S // TILE, block, 0)

        if g == 0:
            break

        def rows(i, carry):
            r = pl.ds(pl.multiple_of(i * TILE, TILE), TILE)

            def emit(cols, value):
                acc[r, cols] = value if index == 0 else acc[r, cols] + value

            products(i, j[r, :], right, emit)
            return carry

        lax.fori_loop(0, S // TILE, rows, 0)

    factor = 1.0 / jnp.sqrt(power[...] / FRAMES + 1e-06)
    power[...] = factor
    for b in range(0, S, 128):
        factor_col[b : b + 128, :] = jnp.broadcast_to(factor[:, b : b + 128], (128, 128)).T

    @pl.when(narrow < NARROW - 1)
    def _():
        sent = x_hbm.at[:, : 2 * L]
        pltpu.make_async_copy(sent, sent, hist_send.at[0]).wait()

    sent = x_hbm.at[:, :L]
    pltpu.make_async_copy(sent, sent, hist_send.at[1]).wait()
    for g in range(CHUNKS):
        part = w.at[g, pl.ds(0, 127)]
        pltpu.make_async_copy(part, part, send_sem).wait()


def finish(acc, last, last_j, factor_row, factor_col, out, stage, sem):
    def arrival(slot):
        return pltpu.make_async_copy(stage.at[slot], out.at[0, pl.ds(0, TILE), :], sem.at[slot])

    def rows(i, slot, wait):
        pl.when(wait)(lambda: arrival(slot).wait())
        r = pl.ds(pl.multiple_of(i * TILE, TILE), TILE)
        scale = jnp.tile(factor_col[r, :], (1, TILE // 128)) * (1.0 / FRAMES)

        def emit(cols, value):
            stage[slot, :, cols] = (acc[r, cols] + value) * scale * factor_row[:, cols]

        products(i, last_j[r, :], last, emit)
        pltpu.make_async_copy(stage.at[slot], out.at[0, r, :], sem.at[slot]).start()

    def both(p, carry):
        rows(2 * p, 0, p > 0)
        rows(2 * p + 1, 1, p > 0)
        return carry

    lax.fori_loop(0, S // TILE // 2, both, 0)
    for slot in range(2):
        arrival(slot).wait()


def body(voltages):
    vmem = pl.BlockSpec(memory_space=pltpu.VMEM)
    hbm = pl.BlockSpec(memory_space=pl.ANY)
    dma = pltpu.SemaphoreType.DMA
    parts = pl.pallas_call(
        exchange,
        out_shape=[
            pltpu.VMEM((S, S), jnp.float32),
            pltpu.VMEM((2, KB, S), jnp.bfloat16),
            pltpu.VMEM((S, KB), jnp.bfloat16),
            pltpu.VMEM((1, S), jnp.float32),
            pltpu.VMEM((S, 128), jnp.float32),
        ],
        in_specs=[hbm, vmem, vmem],
        out_specs=[vmem] * 5,
        scratch_shapes=[
            pltpu.VMEM((ROWS, (FR_DEV + TAPS - 1) * L), jnp.bfloat16),
            pltpu.VMEM((2, 2 * ROWS, L), jnp.bfloat16),
            pltpu.VMEM((STEP * 2 * CHAN, ROWS), jnp.float32),
            pltpu.VMEM((CHUNKS, CHAN, 2 * STEP, ROWS), jnp.bfloat16),
            pltpu.VMEM((CHUNKS - 1, 2, KB, S), jnp.bfloat16),
            pltpu.VMEM((S, KB), jnp.bfloat16),
            pltpu.VMEM((TAPS, L), jnp.float32),
            dma((CHUNKS,)),
            dma((2,)),
            dma((2,)),
            dma,
            dma((CHUNKS,)),
        ],
        compiler_params=pltpu.CompilerParams(
            collective_id=0, has_side_effects=True, vmem_limit_bytes=32 << 20
        ),
        name="exchange",
    )(voltages, taper_table(), channel_table(CHAN).T)
    return pl.pallas_call(
        finish,
        out_shape=jax.ShapeDtypeStruct((1, S, S), jnp.float32),
        in_specs=[vmem] * 5,
        out_specs=hbm,
        scratch_shapes=[pltpu.VMEM((2, TILE, S), jnp.float32), dma((2,))],
        compiler_params=pltpu.CompilerParams(vmem_limit_bytes=6 << 20),
        name="finish",
    )(*parts)


def solution(mesh):
    return jax.shard_map(
        body,
        mesh=mesh,
        in_specs=(P("wide", "narrow"),),
        out_specs=P(("wide", "narrow"), None, None),
        check_vma=False,
    )
```

time: 112 us -> 83.6 us (0.75); the launches traced: 110 us -> 83.5 us
  Pallas kernels: 108 us -> 82.3 us
    pallas_call x2, Pallas kernels: 108 us -> 82.3 us  [the longest x1 73.6 us: body(): pl.pallas_call(exchange, out_shape=[pltpu.VMEM((S, S), jnp.float32), pltp...]
where the time goes in v2:
time: 83.6 us; the launch traced here: 83.5 us
  Pallas kernels  82.3 us (98%)
  other arithmetic  1.21 us (1%)
    pallas_call x1, Pallas kernels, body(): pl.pallas_call(exchange, out_shape=[pltpu.VMEM((S, S), jnp.float32), pltp...  73.6 us
    pallas_call x1, Pallas kernels, body(): pl.pallas_call(finish, out_shape=jax.ShapeDtypeStruct((1, S, S), jnp.floa...  8.63 us

profile of v2, /device:TPU:1, one launch (start us, length us, event | category | flops | bytes accessed | tf_op | source)
XLA Modules:
  0.0 83.5 jit_solution(5264794789373578010)
XLA Ops:
  0.0 0.1 fusion.11.taper
  0.1 1.1 %negate_convert_fusion = (bf16[512,128]{0,1:T(8,128)(2,1)S(1)}, bf16[512,128]{0,1:T(8,128)(2,1)S(1)}) fusion(), kind=kLoop, calls=%fused_computation.7 | loop fusion | flops 1114112 | bytes 262144 | tf_op jit(solution)/shard_map/convert.1
  1.2 73.6 %exchange.1 = (f32[2048,2048]{1,0:T(8,128)S(1)}, bf16[2,256,2048]{2,1,0:T(8,128)(2,1)S(1)}, bf16[2048,256]{1,0:T(8,128)(2,1)S(1)}, f32[1,2048]{1,0:T(1,128)S(1)}, f32[2048,128]{1,0:T(8,128)S(1)}) custom-call(bf16[128,32768]{1,0:T(8,128)(2,1)} %x_hbm.1, f32[4,512]{1,0:T(4,128)S(1)} %fusion.11.taper, bf16[256,512]{1,0:T(8,128)(2,1)S(1)} %maximum_bitcast_fusion.table), custom_call_target="tpu_custom_call" | custom-call | tf_op jit(solution)/shard_map/exchange/pallas_call | solution.py:311
  74.9 8.6 %finish.1 = f32[1,2048,2048]{2,1,0:T(8,128)} custom-call(f32[2048,2048]{1,0:T(8,128)S(1)} %get-tuple-element.10.acc, bf16[2,256,2048]{2,1,0:T(8,128)(2,1)S(1)} %get-tuple-element.11.last, bf16[2048,256]{1,0:T(8,128)(2,1)S(1)} %get-tuple-element.12.last_j, f32[1,2048]{1,0:T(1,128)S(1)} %get-tuple-element.13.factor_row, ...), custom_call_target="tpu_custom_call" | custom-call | tf_op jit(solution)/shard_map/finish/pallas_call | solution.py:341
  (1 shorter events, 0.0 us)

commit v3 on v2

v3 whole, which is shorter than its diff:
```python
import functools
import math

import jax
import jax.numpy as jnp
from jax import lax
from jax.experimental import pallas as pl
from jax.experimental.pallas import tpu as pltpu
from jax.sharding import PartitionSpec as P

S = 2048
L = 512
TAPS = 4
CHAN = 128
FRAMES = 512
WIDE = 16
NARROW = 8
ROWS = S // WIDE
FR_DEV = FRAMES // NARROW
STEP = 16
CHUNKS = FR_DEV // STEP
ORDER = (1, 2, 3, 0)
KB = 2 * STEP * NARROW
TILE = 256
MESH = pl.DeviceIdType.MESH


def channel_table():
    index = lax.broadcasted_iota(jnp.int32, (CHAN, L), 1)
    channel = lax.broadcasted_iota(jnp.int32, (CHAN, L), 0)
    angle = (index * channel % L).astype(jnp.float32) * (2.0 * math.pi / L)
    return jnp.concatenate([jnp.cos(angle), -jnp.sin(angle)], axis=0).astype(jnp.bfloat16)


def taper_table():
    tap = lax.broadcasted_iota(jnp.int32, (TAPS, L), 0)
    place = (tap * L + lax.broadcasted_iota(jnp.int32, (TAPS, L), 1)).astype(jnp.float32)
    offset = (place - TAPS * L / 2.0 + 0.5) * (math.pi / L)
    window = 0.5 - 0.5 * jnp.cos(2.0 * math.pi * (place + 0.5) / (TAPS * L))
    return jnp.sin(offset) / offset * window


def make_chunk(g, xv, taper, taper_edge, table, filt, spec, w):
    def filtered(slot, half, base, weights):
        for r in range(0, ROWS, 16):
            total = None
            for tap in range(TAPS):
                part = xv[r : r + 16, pl.ds(pl.multiple_of(base + tap * L, L), L)]
                term = part.astype(jnp.float32) * weights[tap : tap + 1, :]
                total = term if total is None else total + term
            filt[slot, half * ROWS + r : half * ROWS + r + 16, :] = total.astype(jnp.bfloat16)

    def group(p, carry):
        for slot in range(2):
            for half in range(2):
                f = g * STEP + 4 * p + 2 * slot + half
                filtered(slot, half, jnp.maximum(f - 1, 0) * L, taper)
            if g == 0 and slot == 0:

                @pl.when(p == 0)
                def _():
                    filtered(0, 0, (FR_DEV - 1) * L, taper_edge)

            out = lax.dot_general(
                table[...], filt[slot], (((1,), (1,)), ((), ())), preferred_element_type=jnp.float32
            )
            row = pl.multiple_of((4 * p + 2 * slot) * (2 * CHAN), 2 * 2 * CHAN)
            spec[pl.ds(row, 2 * CHAN), :] = out[:, :ROWS]
            spec[pl.ds(row + 2 * CHAN, 2 * CHAN), :] = out[:, ROWS:]
        return carry

    lax.fori_loop(0, STEP // 4, group, 0)

    def turn(b, carry):
        for c in range(8):
            re = spec[pl.ds(8 * b + c, STEP, stride=2 * CHAN), :]
            im = spec[pl.ds(8 * b + c + CHAN, STEP, stride=2 * CHAN), :]
            w[8 * b + c] = jnp.concatenate([re, im], axis=0).astype(jnp.bfloat16)
        return carry

    lax.fori_loop(0, CHAN // 8, turn, 0)


def prepare(
    x_hbm, xv, taper, table, w, filt, spec, load_sem, send_sem, recv_sem,
):
    wide = lax.axis_index("wide")
    narrow = lax.axis_index("narrow")
    after = (wide, (narrow + 1) % NARROW)
    before = (wide, (narrow + NARROW - 1) % NARROW)
    barrier = pltpu.get_barrier_semaphore()
    for device in (after, before):
        pl.semaphore_signal(barrier, inc=1, device_id=device, device_id_type=MESH)

    first = ORDER[0]
    pieces = [(first * STEP - 3, first * STEP + STEP), (0, first * STEP - 3), (first * STEP + STEP, FR_DEV)]
    loads = [
        pltpu.make_async_copy(
            x_hbm.at[:, begin * L : end * L], xv.at[:, (begin + 2) * L : (end + 2) * L], load_sem.at[index]
        )
        for index, (begin, end) in enumerate(pieces)
    ]
    loads[0].start()
    pl.semaphore_wait(barrier, 2)
    ahead = pltpu.make_async_remote_copy(
        x_hbm.at[:, (FR_DEV - 2) * L :],
        xv.at[:, : 2 * L],
        send_sem.at[0],
        recv_sem.at[0],
        device_id=after,
        device_id_type=MESH,
    )
    back = pltpu.make_async_remote_copy(
        x_hbm.at[:, :L],
        xv.at[:, (FR_DEV + 2) * L :],
        send_sem.at[1],
        recv_sem.at[1],
        device_id=before,
        device_id_type=MESH,
    )
    ahead.start()
    back.start()
    loads[1].start()
    loads[2].start()
    taper[...] = taper_table()
    table[...] = channel_table()
    loads[0].wait()
    make_chunk(first, xv, taper, None, table, filt, spec, w)
    loads[1].wait()
    loads[2].wait()
    ahead.wait()
    back.wait()

    @pl.when(narrow == 0)
    def _():
        xv[:, : 2 * L] = jnp.zeros((ROWS, 2 * L), jnp.bfloat16)


def products(i, left, right, emit):
    def dot(kind, cols):
        return jnp.dot(left, right[kind, :, cols], preferred_element_type=jnp.float32)

    def columns(c):
        return pl.ds(pl.multiple_of(c * TILE, TILE), TILE)

    for t in range(1, S // TILE):
        c = (i + t) % (S // TILE)
        emit(columns(c), dot(jnp.where(c > i, 1, 0), columns(c)))
    row = lax.broadcasted_iota(jnp.int32, (TILE, TILE), 0)
    col = lax.broadcasted_iota(jnp.int32, (TILE, TILE), 1)
    emit(columns(i), jnp.where(row >= col, dot(0, columns(i)), dot(1, columns(i))))


def exchange(
    xv, taper, table, w_first, acc, last, last_j, power, factor_col,
    filt, spec, w, kt, j, taper_edge, send_sem, recv_sem,
):
    wide = lax.axis_index("wide")
    narrow = lax.axis_index("narrow")
    x, y, z, core = wide // 4, (wide // 2) % 2 * 2 + narrow // 4, narrow % 4, wide % 2
    mine = wide * NARROW + narrow

    def partners(q):
        for step in range(4):
            dy = (q % 4 + step) % 4
            px = (x + step) % 4
            py = (y + dy) % 4
            pz = (z + q // 4 + dy + step) % 4
            for flip in range(2):
                pc = (core + flip) % 2
                yield step == 0 and flip == 0, (px * 4 + py // 2 * 2 + pc, py % 2 * 4 + pz)

    def everyone(q, visit):
        for own, device in partners(q):
            if own:
                pl.when(q > 0)(functools.partial(visit, device))
            else:
                visit(device)

    barrier = pltpu.get_barrier_semaphore()

    def greet(q, carry):
        def signal(device):
            pl.semaphore_signal(barrier, inc=1, device_id=device, device_id_type=MESH)

        everyone(q, signal)
        return carry

    lax.fori_loop(0, 16, greet, 0)

    taper_edge[...] = taper[...] * jnp.where(
        (narrow == NARROW - 1) & (lax.broadcasted_iota(jnp.int32, (TAPS, L), 0) < TAPS - 1), 0.0, 1.0
    )

    def chunk(g):
        return w_first if g == ORDER[0] else w.at[ORDER.index(g) - 1]

    def landing(g):
        return kt.at[g - 1, 0] if g > 0 else last.at[0]

    def send(g):
        row = pl.multiple_of(narrow * (2 * STEP), 2 * STEP)
        col = pl.multiple_of(wide * ROWS, ROWS)
        dst = landing(g).at[pl.ds(row, 2 * STEP), pl.ds(col, ROWS)]

        def one(q, carry):
            def start(device):
                pltpu.make_async_remote_copy(
                    chunk(g).at[device[0] * NARROW + device[1]],
                    dst,
                    send_sem,
                    recv_sem.at[g],
                    device_id=device,
                    device_id_type=MESH,
                ).start()

            everyone(q, start)
            return carry

        lax.fori_loop(0, 16, one, 0)
        pltpu.make_async_copy(chunk(g).at[mine], dst, recv_sem.at[g]).start()

    pl.semaphore_wait(barrier, 127)
    send(ORDER[0])
    for g in ORDER[1:]:
        make_chunk(g, xv, taper, taper_edge, table, filt, spec, chunk(g))
        send(g)

    for index, g in enumerate(ORDER):
        right = last if g == 0 else kt.at[g - 1]
        left = last_j if g == 0 else j
        pltpu.make_async_copy(right.at[0], right.at[0], recv_sem.at[g]).wait()

        def block(b, carry):
            cols = pl.ds(pl.multiple_of(b * TILE, TILE), TILE)
            value = right[0, :, cols]
            left[cols, :] = value.T
            sums = jnp.zeros((1, TILE), jnp.float32)
            for r in range(0, KB, 2 * STEP):
                re = value[r : r + STEP, :]
                im = value[r + STEP : r + 2 * STEP, :]
                right[1, r : r + 2 * STEP, cols] = jnp.concatenate([-im, re], axis=0)
                both = value[r : r + 2 * STEP, :].astype(jnp.float32)
                sums = sums + jnp.sum(both * both, axis=0, keepdims=True)
            if index == 0:
                power[:, cols] = sums
            else:
                power[:, cols] = power[:, cols] + sums
            return carry

        lax.fori_loop(0, S // TILE, block, 0)

        if g == 0:
            break

        def rows(i, carry):
            r = pl.ds(pl.multiple_of(i * TILE, TILE), TILE)

            def emit(cols, value):
                acc[r, cols] = value if index == 0 else acc[r, cols] + value

            products(i, j[r, :], right, emit)
            return carry

        lax.fori_loop(0, S // TILE, rows, 0)

    factor = 1.0 / jnp.sqrt(power[...] / FRAMES + 1e-06)
    power[...] = factor
    for b in range(0, S, 128):
        factor_col[b : b + 128, :] = jnp.broadcast_to(factor[:, b : b + 128], (128, 128)).T

    for g in range(CHUNKS):
        part = chunk(g).at[pl.ds(0, 127)]
        pltpu.make_async_copy(part, part, send_sem).wait()


def finish(acc, last, last_j, factor_row, factor_col, out, stage, sem):
    def arrival(slot):
        return pltpu.make_async_copy(stage.at[slot], out.at[0, pl.ds(0, TILE), :], sem.at[slot])

    def rows(i, slot, wait):
        pl.when(wait)(lambda: arrival(slot).wait())
        r = pl.ds(pl.multiple_of(i * TILE, TILE), TILE)
        scale = jnp.tile(factor_col[r, :], (1, TILE // 128)) * (1.0 / FRAMES)

        def emit(cols, value):
            stage[slot, :, cols] = (acc[r, cols] + value) * scale * factor_row[:, cols]

        products(i, last_j[r, :], last, emit)
        pltpu.make_async_copy(stage.at[slot], out.at[0, r, :], sem.at[slot]).start()

    def both(p, carry):
        rows(2 * p, 0, p > 0)
        rows(2 * p + 1, 1, p > 0)
        return carry

    lax.fori_loop(0, S // TILE // 2, both, 0)
    for slot in range(2):
        arrival(slot).wait()


def body(voltages):
    vmem = pl.BlockSpec(memory_space=pltpu.VMEM)
    hbm = pl.BlockSpec(memory_space=pl.ANY)
    dma = pltpu.SemaphoreType.DMA
    work = [
        pltpu.VMEM((2, 2 * ROWS, L), jnp.bfloat16),
        pltpu.VMEM((STEP * 2 * CHAN, ROWS), jnp.float32),
    ]
    prepared = pl.pallas_call(
        prepare,
        out_shape=[
            pltpu.VMEM((ROWS, (FR_DEV + TAPS - 1) * L), jnp.bfloat16),
            pltpu.VMEM((TAPS, L), jnp.float32),
            pltpu.VMEM((2 * CHAN, L), jnp.bfloat16),
            pltpu.VMEM((CHAN, 2 * STEP, ROWS), jnp.bfloat16),
        ],
        in_specs=[hbm],
        out_specs=[vmem] * 4,
        scratch_shapes=[*work, dma((3,)), dma((2,)), dma((2,))],
        compiler_params=pltpu.CompilerParams(
            collective_id=1, has_side_effects=True, vmem_limit_bytes=48 << 20
        ),
        name="prepare",
    )(voltages)
    parts = pl.pallas_call(
        exchange,
        out_shape=[
            pltpu.VMEM((S, S), jnp.float32),
            pltpu.VMEM((2, KB, S), jnp.bfloat16),
            pltpu.VMEM((S, KB), jnp.bfloat16),
            pltpu.VMEM((1, S), jnp.float32),
            pltpu.VMEM((S, 128), jnp.float32),
        ],
        in_specs=[vmem] * 4,
        out_specs=[vmem] * 5,
        scratch_shapes=[
            *work,
            pltpu.VMEM((CHUNKS - 1, CHAN, 2 * STEP, ROWS), jnp.bfloat16),
            pltpu.VMEM((CHUNKS - 1, 2, KB, S), jnp.bfloat16),
            pltpu.VMEM((S, KB), jnp.bfloat16),
            pltpu.VMEM((TAPS, L), jnp.float32),
            dma,
            dma((CHUNKS,)),
        ],
        compiler_params=pltpu.CompilerParams(
            collective_id=0, has_side_effects=True, vmem_limit_bytes=18 << 20
        ),
        name="exchange",
    )(*prepared)
    return pl.pallas_call(
        finish,
        out_shape=jax.ShapeDtypeStruct((1, S, S), jnp.float32),
        in_specs=[vmem] * 5,
        out_specs=hbm,
        scratch_shapes=[pltpu.VMEM((2, TILE, S), jnp.float32), dma((2,))],
        compiler_params=pltpu.CompilerParams(vmem_limit_bytes=6 << 20),
        name="finish",
    )(*parts)


def solution(mesh):
    return jax.shard_map(
        body,
        mesh=mesh,
        in_specs=(P("wide", "narrow"),),
        out_specs=P(("wide", "narrow"), None, None),
        check_vma=False,
    )
```

time: 83.6 us -> 79.6 us (0.952)
  Pallas kernels: 82.3 us -> 79.5 us
  other arithmetic: 1.21 us -> 0 us
    pallas_call x1, Pallas kernels: 73.6 us -> 59.1 us  [body(): pl.pallas_call(exchange, out_shape=[pltpu.VMEM((S, S), jnp.float32), pltp...]
    pallas_call x0 -> x1, Pallas kernels: none -> 11.7 us  [body(): pl.pallas_call(prepare, out_shape=[pltpu.VMEM((ROWS, (FR_DEV + TAPS - 1)...]
    another operation x1 -> x0, other arithmetic: 1.1 us -> none
where the time goes in v3:
time: 79.6 us; the launch traced here: 79.5 us
  Pallas kernels  79.5 us (100%)
    pallas_call x1, Pallas kernels, body(): pl.pallas_call(exchange, out_shape=[pltpu.VMEM((S, S), jnp.float32), pltp...  59.1 us
    pallas_call x1, Pallas kernels, body(): pl.pallas_call(prepare, out_shape=[pltpu.VMEM((ROWS, (FR_DEV + TAPS - 1)...  11.7 us
    pallas_call x1, Pallas kernels, body(): pl.pallas_call(finish, out_shape=jax.ShapeDtypeStruct((1, S, S), jnp.floa...  8.64 us

profile of v3, /device:TPU:1, one launch (start us, length us, event | category | flops | bytes accessed | tf_op | source)
XLA Modules:
  0.0 79.5 jit_solution(10361872230721836806)
XLA Ops:
  0.0 11.7 %prepare.1 = (bf16[128,34304]{1,0:T(8,128)(2,1)S(1)}, f32[4,512]{1,0:T(4,128)S(1)}, bf16[256,512]{1,0:T(8,128)(2,1)S(1)}, bf16[128,32,128]{2,1,0:T(8,128)(2,1)S(1)}) custom-call(bf16[128,32768]{1,0:T(8,128)(2,1)} %x_hbm.1), custom_call_target="tpu_custom_call" | custom-call | tf_op jit(solution)/shard_map/prepare/pallas_call | solution.py:310
  11.7 59.1 %exchange.1 = (f32[2048,2048]{1,0:T(8,128)S(1)}, bf16[2,256,2048]{2,1,0:T(8,128)(2,1)S(1)}, bf16[2048,256]{1,0:T(8,128)(2,1)S(1)}, f32[1,2048]{1,0:T(1,128)S(1)}, f32[2048,128]{1,0:T(8,128)S(1)}) custom-call(bf16[128,34304]{1,0:T(8,128)(2,1)S(1)} %get-tuple-element.14.xv, f32[4,512]{1,0:T(4,128)S(1)} %get-tuple-element.15.taper, ...), custom_call_target="tpu_custom_call" | custom-call | tf_op jit(solution)/shard_map/exchange/pallas_call | solution.py:326
  70.9 8.6 %finish.1 = f32[1,2048,2048]{2,1,0:T(8,128)} custom-call(f32[2048,2048]{1,0:T(8,128)S(1)} %get-tuple-element.18.acc, bf16[2,256,2048]{2,1,0:T(8,128)(2,1)S(1)} %get-tuple-element.19.last, bf16[2048,256]{1,0:T(8,128)(2,1)S(1)} %get-tuple-element.20.last_j, f32[1,2048]{1,0:T(1,128)S(1)} %get-tuple-element.21.factor_row, ...), custom_call_target="tpu_custom_call" | custom-call | tf_op jit(solution)/shard_map/finish/pallas_call | solution.py:351

commit v4 on v3

--- a/solution.py
+++ b/solution.py
@@ -22,6 +22,7 @@
 ORDER = (1, 2, 3, 0)
 KB = 2 * STEP * NARROW
 TILE = 256
+SLOTS = 4
 MESH = pl.DeviceIdType.MESH
 
 
@@ -81,61 +82,6 @@
     lax.fori_loop(0, CHAN // 8, turn, 0)
 
 
-def prepare(
-    x_hbm, xv, taper, table, w, filt, spec, load_sem, send_sem, recv_sem,
-):
-    wide = lax.axis_index("wide")
-    narrow = lax.axis_index("narrow")
-    after = (wide, (narrow + 1) % NARROW)
-    before = (wide, (narrow + NARROW - 1) % NARROW)
-    barrier = pltpu.get_barrier_semaphore()
-    for device in (after, before):
-        pl.semaphore_signal(barrier, inc=1, device_id=device, device_id_type=MESH)
-
-    first = ORDER[0]
-    pieces = [(first * STEP - 3, first * STEP + STEP), (0, first * STEP - 3), (first * STEP + STEP, FR_DEV)]
-    loads = [
-        pltpu.make_async_copy(
-            x_hbm.at[:, begin * L : end * L], xv.at[:, (begin + 2) * L : (end + 2) * L], load_sem.at[index]
-        )
-        for index, (begin, end) in enumerate(pieces)
-    ]
-    loads[0].start()
-    pl.semaphore_wait(barrier, 2)
-    ahead = pltpu.make_async_remote_copy(
-        x_hbm.at[:, (FR_DEV - 2) * L :],
-        xv.at[:, : 2 * L],
-        send_sem.at[0],
-        recv_sem.at[0],
-        device_id=after,
-        device_id_type=MESH,
-    )
-    back = pltpu.make_async_remote_copy(
-        x_hbm.at[:, :L],
-        xv.at[:, (FR_DEV + 2) * L :],
-        send_sem.at[1],
-        recv_sem.at[1],
-        device_id=before,
-        device_id_type=MESH,
-    )
-    ahead.start()
-    back.start()
-    loads[1].start()
-    loads[2].start()
-    taper[...] = taper_table()
-    table[...] = channel_table()
-    loads[0].wait()
-    make_chunk(first, xv, taper, None, table, filt, spec, w)
-    loads[1].wait()
-    loads[2].wait()
-    ahead.wait()
-    back.wait()
-
-    @pl.when(narrow == 0)
-    def _():
-        xv[:, : 2 * L] = jnp.zeros((ROWS, 2 * L), jnp.bfloat16)
-
-
 def products(i, left, right, emit):
     def dot(kind, cols):
         return jnp.dot(left, right[kind, :, cols], preferred_element_type=jnp.float32)
@@ -152,8 +98,8 @@
 
 
 def exchange(
-    xv, taper, table, w_first, acc, last, last_j, power, factor_col,
-    filt, spec, w, kt, j, taper_edge, send_sem, recv_sem,
+    x_hbm, acc, last, last_j, power, factor_col,
+    xv, taper, taper_edge, table, filt, spec, w, kt, j, load_sem, edge_send, edge_recv, send_sem, recv_sem,
 ):
     wide = lax.axis_index("wide")
     narrow = lax.axis_index("narrow")
@@ -188,12 +134,38 @@
 
     lax.fori_loop(0, 16, greet, 0)
 
+    first = ORDER[0]
+    pieces = [(first * STEP - 3, first * STEP + STEP), (first * STEP + STEP, FR_DEV), (0, first * STEP - 3)]
+    loads = [
+        pltpu.make_async_copy(
+            x_hbm.at[:, begin * L : end * L], xv.at[:, (begin + 2) * L : (end + 2) * L], load_sem.at[index]
+        )
+        for index, (begin, end) in enumerate(pieces)
+    ]
+    for copy in loads:
+        copy.start()
+    taper[...] = taper_table()
+    table[...] = channel_table()
     taper_edge[...] = taper[...] * jnp.where(
         (narrow == NARROW - 1) & (lax.broadcasted_iota(jnp.int32, (TAPS, L), 0) < TAPS - 1), 0.0, 1.0
     )
 
-    def chunk(g):
-        return w_first if g == ORDER[0] else w.at[ORDER.index(g) - 1]
+    ahead = pltpu.make_async_remote_copy(
+        x_hbm.at[:, (FR_DEV - 2) * L :],
+        xv.at[:, : 2 * L],
+        edge_send.at[0],
+        edge_recv.at[0],
+        device_id=(wide, (narrow + 1) % NARROW),
+        device_id_type=MESH,
+    )
+    back = pltpu.make_async_remote_copy(
+        x_hbm.at[:, :L],
+        xv.at[:, (FR_DEV + 2) * L :],
+        edge_send.at[1],
+        edge_recv.at[1],
+        device_id=(wide, (narrow + NARROW - 1) % NARROW),
+        device_id_type=MESH,
+    )
 
     def landing(g):
         return kt.at[g - 1, 0] if g > 0 else last.at[0]
@@ -206,7 +178,7 @@
         def one(q, carry):
             def start(device):
                 pltpu.make_async_remote_copy(
-                    chunk(g).at[device[0] * NARROW + device[1]],
+                    w.at[g, device[0] * NARROW + device[1]],
                     dst,
                     send_sem,
                     recv_sem.at[g],
@@ -218,12 +190,23 @@
             return carry
 
         lax.fori_loop(0, 16, one, 0)
-        pltpu.make_async_copy(chunk(g).at[mine], dst, recv_sem.at[g]).start()
+        pltpu.make_async_copy(w.at[g, mine], dst, recv_sem.at[g]).start()
 
     pl.semaphore_wait(barrier, 127)
-    send(ORDER[0])
-    for g in ORDER[1:]:
-        make_chunk(g, xv, taper, taper_edge, table, filt, spec, chunk(g))
+    ahead.start()
+    back.start()
+    for index, g in enumerate(ORDER):
+        if index < len(loads):
+            loads[index].wait()
+        make_chunk(g, xv, taper, taper_edge, table, filt, spec, w.at[g])
+        if index == 0:
+            ahead.wait()
+            back.wait()
+
+            @pl.when(narrow == 0)
+            def _():
+                xv[:, : 2 * L] = jnp.zeros((ROWS, 2 * L), jnp.bfloat16)
+
         send(g)
 
     for index, g in enumerate(ORDER):
@@ -270,7 +253,7 @@
         factor_col[b : b + 128, :] = jnp.broadcast_to(factor[:, b : b + 128], (128, 128)).T
 
     for g in range(CHUNKS):
-        part = chunk(g).at[pl.ds(0, 127)]
+        part = w.at[g, pl.ds(0, 127)]
         pltpu.make_async_copy(part, part, send_sem).wait()
 
 
@@ -289,13 +272,13 @@
         products(i, last_j[r, :], last, emit)
         pltpu.make_async_copy(stage.at[slot], out.at[0, r, :], sem.at[slot]).start()
 
-    def both(p, carry):
-        rows(2 * p, 0, p > 0)
-        rows(2 * p + 1, 1, p > 0)
+    def some(p, carry):
+        for slot in range(SLOTS):
+            rows(SLOTS * p + slot, slot, p > 0)
         return carry
 
-    lax.fori_loop(0, S // TILE // 2, both, 0)
-    for slot in range(2):
+    lax.fori_loop(0, S // TILE // SLOTS, some, 0)
+    for slot in range(SLOTS):
         arrival(slot).wait()
 
 
@@ -303,26 +286,6 @@
     vmem = pl.BlockSpec(memory_space=pltpu.VMEM)
     hbm = pl.BlockSpec(memory_space=pl.ANY)
     dma = pltpu.SemaphoreType.DMA
-    work = [
-        pltpu.VMEM((2, 2 * ROWS, L), jnp.bfloat16),
-        pltpu.VMEM((STEP * 2 * CHAN, ROWS), jnp.float32),
-    ]
-    prepared = pl.pallas_call(
-        prepare,
-        out_shape=[
-            pltpu.VMEM((ROWS, (FR_DEV + TAPS - 1) * L), jnp.bfloat16),
-            pltpu.VMEM((TAPS, L), jnp.float32),
-            pltpu.VMEM((2 * CHAN, L), jnp.bfloat16),
-            pltpu.VMEM((CHAN, 2 * STEP, ROWS), jnp.bfloat16),
-        ],
-        in_specs=[hbm],
-        out_specs=[vmem] * 4,
-        scratch_shapes=[*work, dma((3,)), dma((2,)), dma((2,))],
-        compiler_params=pltpu.CompilerParams(
-            collective_id=1, has_side_effects=True, vmem_limit_bytes=48 << 20
-        ),
-        name="prepare",
-    )(voltages)
     parts = pl.pallas_call(
         exchange,
         out_shape=[
@@ -332,29 +295,36 @@
             pltpu.VMEM((1, S), jnp.float32),
             pltpu.VMEM((S, 128), jnp.float32),
         ],
-        in_specs=[vmem] * 4,
+        in_specs=[hbm],
         out_specs=[vmem] * 5,
         scratch_shapes=[
-            *work,
-            pltpu.VMEM((CHUNKS - 1, CHAN, 2 * STEP, ROWS), jnp.bfloat16),
+            pltpu.VMEM((ROWS, (FR_DEV + TAPS - 1) * L), jnp.bfloat16),
+            pltpu.VMEM((TAPS, L), jnp.float32),
+            pltpu.VMEM((TAPS, L), jnp.float32),
+            pltpu.VMEM((2 * CHAN, L), jnp.bfloat16),
+            pltpu.VMEM((2, 2 * ROWS, L), jnp.bfloat16),
+            pltpu.VMEM((STEP * 2 * CHAN, ROWS), jnp.float32),
+            pltpu.VMEM((CHUNKS, CHAN, 2 * STEP, ROWS), jnp.bfloat16),
             pltpu.VMEM((CHUNKS - 1, 2, KB, S), jnp.bfloat16),
             pltpu.VMEM((S, KB), jnp.bfloat16),
-            pltpu.VMEM((TAPS, L), jnp.float32),
+            dma((3,)),
+            dma((2,)),
+            dma((2,)),
             dma,
             dma((CHUNKS,)),
         ],
         compiler_params=pltpu.CompilerParams(
-            collective_id=0, has_side_effects=True, vmem_limit_bytes=18 << 20
+            collective_id=0, has_side_effects=True, vmem_limit_bytes=40 << 20
         ),
         name="exchange",
-    )(*prepared)
+    )(voltages)
     return pl.pallas_call(
         finish,
         out_shape=jax.ShapeDtypeStruct((1, S, S), jnp.float32),
         in_specs=[vmem] * 5,
         out_specs=hbm,
-        scratch_shapes=[pltpu.VMEM((2, TILE, S), jnp.float32), dma((2,))],
-        compiler_params=pltpu.CompilerParams(vmem_limit_bytes=6 << 20),
+        scratch_shapes=[pltpu.VMEM((SLOTS, TILE, S), jnp.float32), dma((SLOTS,))],
+        compiler_params=pltpu.CompilerParams(vmem_limit_bytes=10 << 20),
         name="finish",
     )(*parts)
 

time: 79.6 us -> 75.6 us (0.950)
  Pallas kernels: 79.5 us -> 75.5 us
    pallas_call x1 -> x0, Pallas kernels: 11.7 us -> none  [body(): pl.pallas_call(prepare, out_shape=[pltpu.VMEM((ROWS, (FR_DEV + TAPS - 1)...]
    pallas_call x1, Pallas kernels: 59.1 us -> 68.9 us  [body(): pl.pallas_call(exchange, out_shape=[pltpu.VMEM((S, S), jnp.float32), pltp...]
    pallas_call x1, Pallas kernels: 8.64 us -> 6.62 us  [body(): pl.pallas_call(finish, out_shape=jax.ShapeDtypeStruct((1, S, S), jnp.floa...]
where the time goes in v4:
time: 75.6 us
  Pallas kernels  75.5 us (100%)
    pallas_call x1, Pallas kernels, body(): pl.pallas_call(exchange, out_shape=[pltpu.VMEM((S, S), jnp.float32), pltp...  68.9 us
    pallas_call x1, Pallas kernels, body(): pl.pallas_call(finish, out_shape=jax.ShapeDtypeStruct((1, S, S), jnp.floa...  6.62 us

profile of v4, /device:TPU:1, one launch (start us, length us, event | category | flops | bytes accessed | tf_op | source)
XLA Modules:
  0.0 75.6 jit_solution(18211454165342718835)
XLA Ops:
  0.0 68.9 %exchange.1 = (f32[2048,2048]{1,0:T(8,128)S(1)}, bf16[2,256,2048]{2,1,0:T(8,128)(2,1)S(1)}, bf16[2048,256]{1,0:T(8,128)(2,1)S(1)}, f32[1,2048]{1,0:T(1,128)S(1)}, f32[2048,128]{1,0:T(8,128)S(1)}) custom-call(bf16[128,32768]{1,0:T(8,128)(2,1)} %x_hbm.1), custom_call_target="tpu_custom_call" | custom-call | tf_op jit(solution)/shard_map/exchange/pallas_call | solution.py:289
  68.9 6.6 %finish.1 = f32[1,2048,2048]{2,1,0:T(8,128)} custom-call(f32[2048,2048]{1,0:T(8,128)S(1)} %get-tuple-element.10.acc, bf16[2,256,2048]{2,1,0:T(8,128)(2,1)S(1)} %get-tuple-element.11.last, bf16[2048,256]{1,0:T(8,128)(2,1)S(1)} %get-tuple-element.12.last_j, f32[1,2048]{1,0:T(1,128)S(1)} %get-tuple-element.13.factor_row, ...), custom_call_target="tpu_custom_call" | custom-call | tf_op jit(solution)/shard_map/finish/pallas_call | solution.py:321

commit v5 on v4

--- a/solution.py
+++ b/solution.py
@@ -41,36 +41,43 @@
     return jnp.sin(offset) / offset * window
 
 
-def make_chunk(g, xv, taper, taper_edge, table, filt, spec, w):
-    def filtered(slot, half, base, weights):
-        for r in range(0, ROWS, 16):
-            total = None
-            for tap in range(TAPS):
-                part = xv[r : r + 16, pl.ds(pl.multiple_of(base + tap * L, L), L)]
-                term = part.astype(jnp.float32) * weights[tap : tap + 1, :]
-                total = term if total is None else total + term
-            filt[slot, half * ROWS + r : half * ROWS + r + 16, :] = total.astype(jnp.bfloat16)
-
+def filtered(xv, filt, slot, half, base, weights, taps=TAPS):
+    for r in range(0, ROWS, 16):
+        total = None
+        for tap in range(taps):
+            part = xv[r : r + 16, pl.ds(pl.multiple_of(base + tap * L, L), L)]
+            term = part.astype(jnp.float32) * weights[tap : tap + 1, :]
+            total = term if total is None else total + term
+        filt[slot, half * ROWS + r : half * ROWS + r + 16, :] = total.astype(jnp.bfloat16)
+
+
+def transformed(table, filt, slot):
+    return lax.dot_general(
+        table[...], filt[slot], (((1,), (1,)), ((), ())), preferred_element_type=jnp.float32
+    )
+
+
+def make_chunk(g, xv, taper, taper_edge, table, filt, spec, w, complete):
     def group(p, carry):
         for slot in range(2):
             for half in range(2):
                 f = g * STEP + 4 * p + 2 * slot + half
-                filtered(slot, half, jnp.maximum(f - 1, 0) * L, taper)
+                filtered(xv, filt, slot, half, jnp.maximum(f - 1, 0) * L, taper)
             if g == 0 and slot == 0:
 
                 @pl.when(p == 0)
                 def _():
-                    filtered(0, 0, (FR_DEV - 1) * L, taper_edge)
-
-            out = lax.dot_general(
-                table[...], filt[slot], (((1,), (1,)), ((), ())), preferred_element_type=jnp.float32
-            )
+                    filtered(xv, filt, 0, 0, (FR_DEV - 1) * L, taper_edge)
+
+            out = transformed(table, filt, slot)
             row = pl.multiple_of((4 * p + 2 * slot) * (2 * CHAN), 2 * 2 * CHAN)
             spec[pl.ds(row, 2 * CHAN), :] = out[:, :ROWS]
             spec[pl.ds(row + 2 * CHAN, 2 * CHAN), :] = out[:, ROWS:]
         return carry
 
     lax.fori_loop(0, STEP // 4, group, 0)
+    if g == 0:
+        complete()
 
     def turn(b, carry):
         for c in range(8):
@@ -99,7 +106,7 @@
 
 def exchange(
     x_hbm, acc, last, last_j, power, factor_col,
-    xv, taper, taper_edge, table, filt, spec, w, kt, j, load_sem, edge_send, edge_recv, send_sem, recv_sem,
+    xv, taper, taper_edge, table, ahead_out, ahead_in, filt, spec, w, kt, j, load_sem, edge_send, edge_recv, send_sem, recv_sem,
 ):
     wide = lax.axis_index("wide")
     narrow = lax.axis_index("narrow")
@@ -135,7 +142,12 @@
     lax.fori_loop(0, 16, greet, 0)
 
     first = ORDER[0]
-    pieces = [(first * STEP - 3, first * STEP + STEP), (first * STEP + STEP, FR_DEV), (0, first * STEP - 3)]
+    pieces = [
+        (FR_DEV - 2, FR_DEV),
+        (first * STEP - 3, first * STEP + STEP),
+        (first * STEP + STEP, FR_DEV - 2),
+        (0, first * STEP - 3),
+    ]
     loads = [
         pltpu.make_async_copy(
             x_hbm.at[:, begin * L : end * L], xv.at[:, (begin + 2) * L : (end + 2) * L], load_sem.at[index]
@@ -144,6 +156,7 @@
     ]
     for copy in loads:
         copy.start()
+    xv[:, : 2 * L] = jnp.zeros((ROWS, 2 * L), jnp.bfloat16)
     taper[...] = taper_table()
     table[...] = channel_table()
     taper_edge[...] = taper[...] * jnp.where(
@@ -151,8 +164,8 @@
     )
 
     ahead = pltpu.make_async_remote_copy(
-        x_hbm.at[:, (FR_DEV - 2) * L :],
-        xv.at[:, : 2 * L],
+        ahead_out,
+        ahead_in,
         edge_send.at[0],
         edge_recv.at[0],
         device_id=(wide, (narrow + 1) % NARROW),
@@ -192,21 +205,29 @@
         lax.fori_loop(0, 16, one, 0)
         pltpu.make_async_copy(w.at[g, mine], dst, recv_sem.at[g]).start()
 
+    loads[0].wait()
+    filtered(xv, filt, 0, 0, FR_DEV * L, taper, 2)
+    filtered(xv, filt, 0, 1, (FR_DEV + 1) * L, taper, 1)
+    out = transformed(table, filt, 0).astype(jnp.bfloat16)
+    ahead_out[: 2 * CHAN, :] = out[:, :ROWS]
+    ahead_out[2 * CHAN :, :] = out[:, ROWS:]
+
+    def complete():
+        @pl.when(narrow > 0)
+        def _():
+            rows = slice(2 * CHAN, 3 * 2 * CHAN)
+            spec[rows, :] = spec[rows, :] + ahead_in[...].astype(jnp.float32)
+
     pl.semaphore_wait(barrier, 127)
     ahead.start()
     back.start()
     for index, g in enumerate(ORDER):
-        if index < len(loads):
-            loads[index].wait()
-        make_chunk(g, xv, taper, taper_edge, table, filt, spec, w.at[g])
-        if index == 0:
+        if index + 1 < len(loads):
+            loads[index + 1].wait()
+        if g == 0:
             ahead.wait()
             back.wait()
-
-            @pl.when(narrow == 0)
-            def _():
-                xv[:, : 2 * L] = jnp.zeros((ROWS, 2 * L), jnp.bfloat16)
-
+        make_chunk(g, xv, taper, taper_edge, table, filt, spec, w.at[g], complete)
         send(g)
 
     for index, g in enumerate(ORDER):
@@ -302,12 +323,14 @@
             pltpu.VMEM((TAPS, L), jnp.float32),
             pltpu.VMEM((TAPS, L), jnp.float32),
             pltpu.VMEM((2 * CHAN, L), jnp.bfloat16),
+            pltpu.VMEM((2 * 2 * CHAN, ROWS), jnp.bfloat16),
+            pltpu.VMEM((2 * 2 * CHAN, ROWS), jnp.bfloat16),
             pltpu.VMEM((2, 2 * ROWS, L), jnp.bfloat16),
             pltpu.VMEM((STEP * 2 * CHAN, ROWS), jnp.float32),
             pltpu.VMEM((CHUNKS, CHAN, 2 * STEP, ROWS), jnp.bfloat16),
             pltpu.VMEM((CHUNKS - 1, 2, KB, S), jnp.bfloat16),
             pltpu.VMEM((S, KB), jnp.bfloat16),
-            dma((3,)),
+            dma((4,)),
             dma((2,)),
             dma((2,)),
             dma,

time: 75.6 us -> 72.1 us (0.954)
  Pallas kernels: 75.5 us -> 72 us
    pallas_call x1, Pallas kernels: 68.9 us -> 65.4 us  [body(): pl.pallas_call(exchange, out_shape=[pltpu.VMEM((S, S), jnp.float32), pltp...]
where the time goes in v5:
time: 72.1 us; the launch traced here: 72 us
  Pallas kernels  72 us (100%)
    pallas_call x1, Pallas kernels, body(): pl.pallas_call(exchange, out_shape=[pltpu.VMEM((S, S), jnp.float32), pltp...  65.4 us
    pallas_call x1, Pallas kernels, body(): pl.pallas_call(finish, out_shape=jax.ShapeDtypeStruct((1, S, S), jnp.floa...  6.65 us

profile of v5, /device:TPU:1, one launch (start us, length us, event | category | flops | bytes accessed | tf_op | source)
XLA Modules:
  0.0 72.0 jit_solution(5432099029580431765)
XLA Ops:
  0.0 65.4 %exchange.1 = (f32[2048,2048]{1,0:T(8,128)S(1)}, bf16[2,256,2048]{2,1,0:T(8,128)(2,1)S(1)}, bf16[2048,256]{1,0:T(8,128)(2,1)S(1)}, f32[1,2048]{1,0:T(1,128)S(1)}, f32[2048,128]{1,0:T(8,128)S(1)}) custom-call(bf16[128,32768]{1,0:T(8,128)(2,1)} %x_hbm.1), custom_call_target="tpu_custom_call" | custom-call | tf_op jit(solution)/shard_map/exchange/pallas_call | solution.py:310
  65.4 6.6 %finish.1 = f32[1,2048,2048]{2,1,0:T(8,128)} custom-call(f32[2048,2048]{1,0:T(8,128)S(1)} %get-tuple-element.10.acc, bf16[2,256,2048]{2,1,0:T(8,128)(2,1)S(1)} %get-tuple-element.11.last, bf16[2048,256]{1,0:T(8,128)(2,1)S(1)} %get-tuple-element.12.last_j, f32[1,2048]{1,0:T(1,128)S(1)} %get-tuple-element.13.factor_row, ...), custom_call_target="tpu_custom_call" | custom-call | tf_op jit(solution)/shard_map/finish/pallas_call | solution.py:344

commit v6 on v5

--- a/solution.py
+++ b/solution.py
@@ -218,9 +218,6 @@
             rows = slice(2 * CHAN, 3 * 2 * CHAN)
             spec[rows, :] = spec[rows, :] + ahead_in[...].astype(jnp.float32)
 
-    pl.semaphore_wait(barrier, 127)
-    ahead.start()
-    back.start()
     for index, g in enumerate(ORDER):
         if index + 1 < len(loads):
             loads[index + 1].wait()
@@ -228,6 +225,10 @@
             ahead.wait()
             back.wait()
         make_chunk(g, xv, taper, taper_edge, table, filt, spec, w.at[g], complete)
+        if index == 0:
+            pl.semaphore_wait(barrier, 127)
+            ahead.start()
+            back.start()
         send(g)
 
     for index, g in enumerate(ORDER):

time: 72.1 us -> 82.2 us (1.14)
  the two profiles are of different devices: /device:TPU:1 before, /device:TPU:16 now
where the time goes in v6:
time: 82.2 us; the launch traced here: 82.1 us
  Pallas kernels  82 us (100%)
    pallas_call x1, Pallas kernels, body(): pl.pallas_call(exchange, out_shape=[pltpu.VMEM((S, S), jnp.float32), pltp...  75.4 us
    pallas_call x1, Pallas kernels, body(): pl.pallas_call(finish, out_shape=jax.ShapeDtypeStruct((1, S, S), jnp.floa...  6.62 us

profile of v6, /device:TPU:16, one launch (start us, length us, event | category | flops | bytes accessed | tf_op | source)
XLA Modules:
  0.0 82.1 jit_solution(3705385526207472056)
XLA Ops:
  0.0 75.4 %exchange.1 = (f32[2048,2048]{1,0:T(8,128)S(1)}, bf16[2,256,2048]{2,1,0:T(8,128)(2,1)S(1)}, bf16[2048,256]{1,0:T(8,128)(2,1)S(1)}, f32[1,2048]{1,0:T(1,128)S(1)}, f32[2048,128]{1,0:T(8,128)S(1)}) custom-call(bf16[128,32768]{1,0:T(8,128)(2,1)} %x_hbm.1), custom_call_target="tpu_custom_call" | custom-call | tf_op jit(solution)/shard_map/exchange/pallas_call | solution.py:311
  75.4 6.6 %finish.1 = f32[1,2048,2048]{2,1,0:T(8,128)} custom-call(f32[2048,2048]{1,0:T(8,128)S(1)} %get-tuple-element.10.acc, bf16[2,256,2048]{2,1,0:T(8,128)(2,1)S(1)} %get-tuple-element.11.last, bf16[2048,256]{1,0:T(8,128)(2,1)S(1)} %get-tuple-element.12.last_j, f32[1,2048]{1,0:T(1,128)S(1)} %get-tuple-element.13.factor_row, ...), custom_call_target="tpu_custom_call" | custom-call | tf_op jit(solution)/shard_map/finish/pallas_call | solution.py:345
